TPU v7x, 32 devices: a whole 2x2x4 slice. The times are simulated.
32 devices in a mesh: groups: 2 (over y), sec: 4 (over z), op: 4 (over x, core).
Axes of the slice: x: 2, y: 2, z: 4, core: 2. Of those that a mesh axis runs over, the one named last changes fastest.
Arguments:
- psi: bfloat16 [224, 128, 256], P(('groups', 'sec')), parts along dimension 0, may hold values from -6 to 6
- left_ops: bfloat16 [4, 56, 128, 128], P('op', ('groups', 'sec')), parts along dimension 1, may hold values from -0.25 to 0.25
- right_ops: bfloat16 [4, 56, 256, 256], P('op', ('groups', 'sec')), parts along dimension 1, may hold values from -0.375 to 0.375
- left_dims: int32 [56], P('groups'), parts along dimension 0, may hold values from 32 to 128, as said below
- right_dims: int32 [56], P('groups'), parts along dimension 0, may hold values from 64 to 256, as said below
- block_left: int32 [224], P('groups'), parts along dimension 0, may hold values from 0 to 6
- block_right: int32 [224], P('groups'), parts along dimension 0, may hold values from 0 to 6
- right_owner: int32 [224], P('groups'), parts along dimension 0, may hold values from 0 to 3, as said below
Outputs:
- sigma_first: bfloat16 [224, 128, 256], P(('groups', 'sec'), 'op'), parts along dimension 0
- sigma_second: bfloat16 [224, 128, 256], P(('groups', 'sec'), 'op'), parts along dimension 0
There are 2 independent parts, one for each index of `groups`. A program takes and returns all parts, laid end to end along the dimension named above; each array names one. Nothing has to cross between parts.
Inputs may be any that keep to these rules, and one draw needn't show every extreme that they name: `left_dims`: some left sector has dimension 128. `right_dims`: some right sector has dimension 256. `right_owner`: among the 28 blocks of one left owner (blocks j * 28 to (j + 1) * 28 - 1) no right owner appears more than 7 times, and some appears exactly 7 times.
All inputs are finite; a program needn't handle non-finite values.
Results may differ from a plain program's by a relative error of at most 0.017.
Values may be sent and summed in bfloat16 or wider, within the bound.
A program may use at most 64 MiB of HBM per device.

v0:
```python
import jax
import jax.numpy as jnp
from jax import lax
from jax.sharding import PartitionSpec as P


def block_masks(row_count, col_count, left_dim, right_dim):
    row_ids = lax.broadcasted_iota(jnp.int32, (1, row_count, 1), 1)
    col_ids = lax.broadcasted_iota(jnp.int32, (1, 1, col_count), 2)
    return (row_ids < left_dim[:, None, None]) & (col_ids < right_dim[:, None, None])


def left_apply(matrices, values):
    return jnp.einsum("pra,pac->prc", matrices, values, preferred_element_type=jnp.float32).astype(
        jnp.bfloat16
    )


def right_apply(matrices, values):
    return jnp.einsum("prc,pdc->prd", values, matrices, preferred_element_type=jnp.float32).astype(
        jnp.bfloat16
    )


def op_combine(terms, live_mask, row_share, op_index):
    own_rows = lax.psum_scatter(
        terms.astype(jnp.bfloat16), "op", scatter_dimension=1, tiled=True
    ).astype(jnp.float32)
    own_mask = lax.dynamic_slice_in_dim(live_mask, op_index * row_share, row_share, 1)
    own_rows = jnp.where(own_mask, own_rows, 0.0).astype(jnp.bfloat16)
    full_sigma = lax.all_gather(own_rows, "op", axis=1, tiled=True)
    return (full_sigma, own_rows)


def body(psi, left_ops, right_ops, left_dims, right_dims, block_left, block_right, right_owner):
    senders = lax.axis_size("sec")
    holders = lax.axis_size("op")
    my_index = lax.axis_index("sec")
    op_index = lax.axis_index("op")
    block_count, left_rows, right_cols = psi.shape
    peer_slots = -(-block_count // senders)
    buffer_len = senders * peer_slots
    left_per = left_ops.shape[1]
    right_per = right_ops.shape[1]
    row_share = left_rows // holders
    owner_table = right_owner.reshape(senders, block_count)
    same_owner = owner_table[:, :, None] == owner_table[:, None, :]
    earlier = lax.broadcasted_iota(jnp.int32, (block_count, block_count), 1) < lax.broadcasted_iota(
        jnp.int32, (block_count, block_count), 0
    )
    order_rank = jnp.sum((same_owner & earlier[None]).astype(jnp.int32), axis=2)
    sender_ids = lax.broadcasted_iota(jnp.int32, (senders, block_count), 0)
    mine_owner = lax.dynamic_index_in_dim(owner_table, my_index, 0, keepdims=False)
    mine_rank = lax.dynamic_index_in_dim(order_rank, my_index, 0, keepdims=False)
    send_pos = mine_owner * peer_slots + mine_rank
    mine_left = lax.dynamic_slice_in_dim(block_left, my_index * block_count, block_count)
    mine_right = lax.dynamic_slice_in_dim(block_right, my_index * block_count, block_count)
    left_mask = block_masks(
        left_rows,
        right_cols,
        left_dims[my_index * left_per + mine_left],
        right_dims[mine_owner * right_per + mine_right],
    )
    slot_ids = jnp.arange(buffer_len, dtype=jnp.int32)
    recv_pos = (sender_ids * peer_slots + order_rank).reshape(-1)
    recv_select = (right_owner == my_index)[None, :] & (recv_pos[None, :] == slot_ids[:, None])
    recv_right = jnp.sum(jnp.where(recv_select, block_right[None, :], 0), axis=1)
    right_matrices = right_ops[0][recv_right]
    left_matrices = left_ops[0][mine_left]
    inputs = jnp.where(left_mask, psi, jnp.zeros_like(psi))
    first_terms = left_apply(left_matrices, inputs)
    operators_back = lax.all_to_all(right_matrices, "sec", split_axis=0, concat_axis=0, tiled=True)
    mine_matrices = jnp.take(operators_back, send_pos, axis=0)
    partial_terms = right_apply(mine_matrices, first_terms)
    full_sigma, sigma_first = op_combine(
        partial_terms.astype(jnp.float32), left_mask, row_share, op_index
    )
    second_terms = left_apply(left_matrices, right_apply(mine_matrices, full_sigma))
    final_rows = lax.psum_scatter(
        second_terms.astype(jnp.float32).astype(jnp.bfloat16), "op", scatter_dimension=1, tiled=True
    ).astype(jnp.float32)
    final_mask = lax.dynamic_slice_in_dim(left_mask, op_index * row_share, row_share, 1)
    sigma_second = jnp.where(final_mask, final_rows, 0.0).astype(jnp.bfloat16)
    return (sigma_first, sigma_second)


def solution(mesh):
    return jax.shard_map(
        body,
        mesh=mesh,
        in_specs=(
            P(("groups", "sec"), None, None),
            P("op", ("groups", "sec"), None, None),
            P("op", ("groups", "sec"), None, None),
            P("groups"),
            P("groups"),
            P("groups"),
            P("groups"),
            P("groups"),
        ),
        out_specs=(P(("groups", "sec"), "op", None), P(("groups", "sec"), "op", None)),
        check_vma=False,
    )
```

profile of v0, /device:TPU:0, one launch (start us, length us, event | category | flops | bytes accessed | tf_op | source)
XLA Modules:
  0.0 208.8 jit_solution(9248443458059982560)
XLA Ops:
  7.2 0.0 copy-start
  7.2 0.8 reshape.131
  8.0 0.7 broadcast_compare_fusion
  8.7 0.1 copy.16
  8.8 0.6 convert_reduce_fusion
  9.4 0.1 copy.18
  9.5 0.1 broadcast_add_fusion
  9.6 0.1 add.99
  9.7 0.8 select_reduce_fusion
  10.5 0.0 copy-done
  10.5 2.6 %gather_fusion.3 = bf16[28,256,256]{2,1,0:T(8,128)(2,1)} fusion(bf16[7,256,256]{2,1,0:T(8,128)(2,1)S(1)} %bitcast.13, s32[1024]{0:T(1024)S(1)} %pad_clamp_fusion.1), kind=kCustom, calls=%fused_computation.3 | custom fusion | bytes 7340144 | tf_op jit(solution)/shard_map/gather | solution.py:68
  13.1 0.0 copy-start.4
  13.1 0.0 copy-start.5
  13.1 0.0 copy-start.1
  13.1 0.0 copy-start.2
  13.1 0.0 copy-start.3
  13.1 6.5 %all-to-all-start = ((bf16[28,256,256]{2,1,0:T(8,128)(2,1)}), bf16[28,256,256]{2,1,0:T(8,128)(2,1)}, u32[]{:S(2)}, u32[]{:S(2)}) async-start(bf16[28,256,256]{2,1,0:T(8,128)(2,1)} %gather_fusion.3), calls=%async_computation | async-start | bytes 7340032 | tf_op jit(solution)/shard_map/all_to_all | solution.py:72
  19.6 0.0 reduce-scatter.3.cloned.1.call-start
  19.6 0.2 dynamic-slice_reduce_fusion
  19.8 0.0 copy-done.4
  19.8 0.0 copy-done.5
  19.8 0.1 compare_select_fusion.5
  19.9 0.0 copy-done.1
  19.9 0.7 gather_fusion
  20.6 0.0 copy-done.2
  20.6 0.7 gather_fusion.1
  21.3 0.0 copy-done.3
  21.4 0.7 gather_fusion.2
  22.1 0.1 iota_compare_fusion.3
  22.2 0.1 iota_compare_fusion
  22.3 79.4 %all-to-all-done = bf16[28,256,256]{2,1,0:T(8,128)(2,1)} async-done(((bf16[28,256,256]{2,1,0:T(8,128)(2,1)}), bf16[28,256,256]{2,1,0:T(8,128)(2,1)}, u32[]{:S(2)}, u32[]{:S(2)}) %all-to-all-start) | async-done | bytes 3670048 | tf_op jit(solution)/shard_map/all_to_all | solution.py:72
  101.7 4.7 %gather_fusion.4 = bf16[28,256,256]{2,1,0:T(8,128)(2,1)} fusion(bf16[28,256,256]{2,1,0:T(8,128)(2,1)} %all-to-all-done, s32[1024]{0:T(1024)S(1)} %pad_clamp_fusion), kind=kCustom, calls=%fused_computation.4 | custom fusion | bytes 7340144 | tf_op jit(solution)/shard_map/jit(_take)/gather | solution.py:73
  106.4 5.8 %fusion.10 = bf16[28,128,256]{2,1,0:T(8,128)(2,1)} fusion(bf16[28,128,128]{2,1,0:T(8,128)(2,1)S(1)} %gather_fusion.2, bf16[28,128,256]{2,1,0:T(8,128)(2,1)} %param.8, bf16[28,256,256]{2,1,0:T(8,128)(2,1)} %gather_fusion.4, pred[28]{0:T(512)(128)(4,1)S(1)} %compare_and_fusion, pred[28,256]{1,0:T(8,128)(4,1)S(1)} %iota_compare_fusion, ...), kind=kOutput, calls=%fused_computation.14 | convolution fusion | flops 710148096 | bytes 8268316 | tf_op jit(solution)/shard_map/prc,pdc->prd/dot_general | solution.py:20
  112.1 0.0 reduce-scatter.3.cloned.1.call-update
  112.2 0.0 all-gather.2.cloned.1.call-start
  112.2 0.7 broadcast_and_fusion
  113.0 28.3 %reduce-scatter.3.cloned.1.call-done = bf16[28,32,256]{2,1,0:T(8,128)(2,1)} async-done(((bf16[28,128,256]{2,1,0:T(8,128)(2,1)}), bf16[28,32,256]{2,1,0:T(8,128)(2,1)}) %reduce-scatter.3.cloned.1.call-update) | async-done | bytes 458768 | tf_op jit(solution)/shard_map/reduce_scatter | solution.py:26
  141.2 1.9 select_convert_fusion.1
  143.2 0.0 all-gather.2.cloned.1.call-update
  143.2 0.0 reduce-scatter.5.cloned.1.call-start
  143.2 21.4 %all-gather.2.cloned.1.call-done = bf16[28,128,256]{2,1,0:T(8,128)(2,1)} async-done(((bf16[28,32,256]{2,1,0:T(8,128)(2,1)}), bf16[28,128,256]{2,1,0:T(8,128)(2,1)}) %all-gather.2.cloned.1.call-update) | async-done | bytes 1835024 | tf_op jit(solution)/shard_map/all_gather | solution.py:31
  164.6 5.7 %fusion.15 = bf16[28,128,256]{2,1,0:T(8,128)(2,1)} fusion(bf16[28,128,128]{2,1,0:T(8,128)(2,1)S(1)} %gather_fusion.2, bf16[28,128,256]{2,1,0:T(8,128)(2,1)} %all-gather.2.cloned.1.call-done, bf16[28,256,256]{2,1,0:T(8,128)(2,1)} %gather_fusion.4, pred[28]{0:T(512)(128)(4,1)S(1)} %compare_and_fusion), kind=kOutput, calls=%fused_computation.15 | convolution fusion | flops 708313088 | bytes 8257564 | tf_op jit(solution)/shard_map/pra,pac->prc/dot_general | solution.py:14
  170.3 0.0 reduce-scatter.5.cloned.1.call-update
  170.4 30.0 %reduce-scatter.5.cloned.1.call-done = bf16[28,32,256]{2,1,0:T(8,128)(2,1)} async-done(((bf16[28,128,256]{2,1,0:T(8,128)(2,1)}), bf16[28,32,256]{2,1,0:T(8,128)(2,1)}) %reduce-scatter.5.cloned.1.call-update) | async-done | bytes 458768 | tf_op jit(solution)/shard_map/reduce_scatter | solution.py:79
  200.3 1.9 select_convert_fusion
  (10 shorter events, 0.1 us)
Async XLA Ops:
  7.2 3.3 %copy-start = (bf16[1,7,256,256]{3,2,1,0:T(8,128)(2,1)S(1)}, bf16[1,7,256,256]{3,2,1,0:T(8,128)(2,1)}, u32[]{:S(2)}) copy-start(bf16[1,7,256,256]{3,2,1,0:T(8,128)(2,1)} %param.10) | copy-start | bytes 2752516
  13.1 6.7 %copy-start.4 = (s32[112]{0:T(128)S(1)}, s32[112]{0:T(128)}, u32[]{:S(2)}) copy-start(s32[112]{0:T(128)} %param.14) | copy-start | bytes 1348
  13.1 6.7 %copy-start.5 = (s32[112]{0:T(128)S(1)}, s32[112]{0:T(128)}, u32[]{:S(2)}) copy-start(s32[112]{0:T(128)} %param.13) | copy-start | bytes 1348
  13.1 6.8 %copy-start.1 = (s32[28]{0:T(128)S(1)}, s32[28]{0:T(128)}, u32[]{:S(2)}) copy-start(s32[28]{0:T(128)} %param.11) | copy-start | bytes 340
  13.1 7.5 %copy-start.2 = (s32[28]{0:T(128)S(1)}, s32[28]{0:T(128)}, u32[]{:S(2)}) copy-start(s32[28]{0:T(128)} %param.12) | copy-start | bytes 340
  13.1 8.2 %copy-start.3 = (bf16[1,7,128,128]{3,2,1,0:T(8,128)(2,1)S(1)}, bf16[1,7,128,128]{3,2,1,0:T(8,128)(2,1)}, u32[]{:S(2)}) copy-start(bf16[1,7,128,128]{3,2,1,0:T(8,128)(2,1)} %param.9) | copy-start | bytes 688132
  13.1 88.6 %all-to-all-start = ((bf16[28,256,256]{2,1,0:T(8,128)(2,1)}), bf16[28,256,256]{2,1,0:T(8,128)(2,1)}, u32[]{:S(2)}, u32[]{:S(2)}) async-start(bf16[28,256,256]{2,1,0:T(8,128)(2,1)} %gather_fusion.3), calls=%async_computation | async-start | bytes 7340032 | tf_op jit(solution)/shard_map/all_to_all | solution.py:72
  19.6 121.6 %reduce-scatter.3.cloned.1.call-start = ((), (), s32[]{:S(2)}) async-start(), calls=%async_computation.3 | async-start | bytes 2293760 | tf_op jit(solution)/shard_map/reduce_scatter | solution.py:26
  112.2 52.4 %all-gather.2.cloned.1.call-start = ((), (), s32[]{:S(2)}) async-start(), calls=%async_computation.4 | async-start | bytes 2293760 | tf_op jit(solution)/shard_map/all_gather | solution.py:31
  143.2 57.2 %reduce-scatter.5.cloned.1.call-start = ((), (), s32[]{:S(2)}) async-start(), calls=%async_computation.5 | async-start | bytes 2293760 | tf_op jit(solution)/shard_map/reduce_scatter | solution.py:79
Sparse Core Ops, SparseCore 0:
  112.3 28.8 reduce-scatter.2
  143.4 21.1 all-gather.1
  170.5 29.8 reduce-scatter.4
where the time goes:
time: 209 us
  waiting for transfers between devices  159 us (76%)
  between operations  13.9 us (7%)
  matrix products  11.5 us (6%)
  local copies, waits for them, and re-layouts  10.5 us (5%)
  other arithmetic  7.23 us (3%)
  starting transfers between devices  6.55 us (3%)
    all_to_all x1, waiting for transfers between devices, body(): lax.all_to_all(right_matrices, 'sec', split_axis=0, concat_axis=0, tiled=...  79.4 us
    reduce_scatter x1, waiting for transfers between devices, body(): lax.psum_scatter(second_terms.astype(jnp.float32).astype(jnp.bfloat16), '...  30 us
    reduce_scatter x1, waiting for transfers between devices, op_combine(): lax.psum_scatter(terms.astype(jnp.bfloat16), 'op', scatter_dimension=1, t...  28.3 us
    all_gather x1, waiting for transfers between devices, op_combine(): full_sigma = lax.all_gather(own_rows, 'op', axis=1, tiled=True)  21.4 us
    all_to_all x1, starting transfers between devices, body(): lax.all_to_all(right_matrices, 'sec', split_axis=0, concat_axis=0, tiled=...  6.46 us
    dot_general x1, matrix products, right_apply(): jnp.einsum('prc,pdc->prd', values, matrices, preferred_element_type=jnp.f...  5.78 us
    dot_general x1, matrix products, left_apply(): jnp.einsum('pra,pac->prc', matrices, values, preferred_element_type=jnp.f...  5.74 us
    gather x1, local copies, waits for them, and re-layouts, body(): mine_matrices = jnp.take(operators_back, send_pos, axis=0)  4.67 us
  transfers between devices with their start and end apart: 4, of which 4 were waited for; matrix products, arithmetic and copies ran while one was open for 2% of the time, Pallas kernels for 0%

commit v1 on v0

--- a/solution.py
+++ b/solution.py
@@ -1,6 +1,10 @@
+import functools
+
 import jax
 import jax.numpy as jnp
 from jax import lax
+from jax.experimental import pallas as pl
+from jax.experimental.pallas import tpu as pltpu
 from jax.sharding import PartitionSpec as P
 
 
@@ -84,9 +88,362 @@
     return (sigma_first, sigma_second)
 
 
+MESH = pl.DeviceIdType.MESH
+CORES = 2
+SKEW = 2
+VMEM_BUDGET = 40 * 2**20
+
+
+def kernel(
+    senders,
+    holders,
+    send_block,
+    recv_block,
+    send_place,
+    left_dims,
+    right_dims,
+    block_left,
+    block_right,
+    psi,
+    left_ops,
+    right_ops,
+    out_first,
+    out_second,
+    packed,
+    values,
+    partial,
+    from_core,
+    to_chip,
+    from_chip,
+    final,
+    returned_first,
+    returned_second,
+    z_send,
+    z_recv,
+    agx_send,
+    agx_recv,
+    agc_send,
+    agc_recv,
+    rsc_send,
+    rsc_recv,
+    rsx_send,
+    rsx_recv,
+    *left_recv,
+):
+    me = lax.axis_index("sec")
+    op = lax.axis_index("op")
+    chips = holders // CORES
+    chip, core = op // CORES, op % CORES
+    blocks, rows, cols = psi.shape
+    left_per, right_per = left_ops.shape[0], right_ops.shape[0]
+    slots = values.shape[2]
+    share = rows // holders
+    returned = (returned_first, returned_second)
+
+    def share_rows(chip_index, core_index):
+        start = (chip_index * CORES + core_index) * share
+        return pl.ds(pl.multiple_of(start, share), share)
+
+    own_rows = share_rows(chip, core)
+    partner = {"op": chip * CORES + (1 - core)}
+    chip_at = [lax.rem(chip + e, chips) for e in range(chips)]
+    chip_peer = [{"op": c * CORES + core} for c in chip_at]
+    sec_before = [lax.rem(me - d + senders, senders) for d in range(senders)]
+    sec_after = [lax.rem(me + d, senders) for d in range(senders)]
+
+    barrier = pltpu.get_barrier_semaphore()
+    peers = [{"sec": sec_before[d]} for d in range(1, senders)] + [partner] + chip_peer[1:]
+    for peer in peers:
+        pl.semaphore_signal(barrier, inc=1, device_id=peer, device_id_type=MESH)
+
+    row_ids = lax.broadcasted_iota(jnp.int32, (share, cols), 0) + op * share
+    col_ids = lax.broadcasted_iota(jnp.int32, (share, cols), 1)
+
+    def pack(d):
+        def one(k, carry):
+            block = send_block[d * slots + k]
+            value = psi[block, own_rows, :].astype(jnp.float32)
+            gb = me * blocks + block
+            row_limit = left_dims[me * left_per + block_left[gb]]
+            col_limit = right_dims[sec_before[d] * right_per + block_right[gb]]
+            live = (row_ids < row_limit) & (col_ids < col_limit)
+            value = jnp.where(live, value, 0.0).astype(jnp.bfloat16)
+            if d == 0:
+                values[0, 0, k, own_rows, :] = value
+            else:
+                packed[d, k] = value
+            return carry
+
+        lax.fori_loop(0, slots, one, 0, unroll=True)
+
+    def remote(src, dst, send_sem, recv_sem, device):
+        copy = pltpu.make_async_remote_copy(
+            src_ref=src,
+            dst_ref=dst,
+            send_sem=send_sem,
+            recv_sem=recv_sem,
+            device_id=device,
+            device_id_type=MESH,
+        )
+        copy.start()
+        sent.append(copy)
+        return copy
+
+    sent = []
+    inbound, left_in, gather_chip, gather_core, reduce_core, reduce_chip, back = (
+        {},
+        {},
+        {},
+        {},
+        {},
+        {},
+        {},
+    )
+
+    for d in range(senders):
+        pack(d)
+    pl.semaphore_wait(barrier, len(peers))
+    for d in range(1, senders):
+        to = {"sec": sec_before[d]}
+        inbound[d] = remote(
+            packed.at[d],
+            values.at[0, d, :, own_rows, :],
+            z_send.at[0, d],
+            z_recv.at[0, d],
+            to,
+        )
+        left_in[d] = remote(left_ops, left_recv[d - 1], z_send.at[1, d], z_recv.at[1, d], to)
+
+    def gather_start(t, d):
+        if t == 0 and d > 0:
+            inbound[d].wait_recv()
+        part = values.at[t, d, :, own_rows, :]
+        for e in range(1, chips):
+            gather_chip[t, d, e] = remote(
+                part, part, agx_send.at[t, d, e], agx_recv.at[t, d, e], chip_peer[e]
+            )
+        gather_core[t, d, 0] = remote(
+            part, part, agc_send.at[t, d, 0], agc_recv.at[t, d, 0], partner
+        )
+
+    def gather_pass(t, d):
+        for e in range(1, chips):
+            gather_chip[t, d, e].wait_recv()
+            part = values.at[t, d, :, share_rows(chip_at[chips - e], core), :]
+            gather_core[t, d, e] = remote(
+                part, part, agc_send.at[t, d, e], agc_recv.at[t, d, e], partner
+            )
+
+    def apply(t, d):
+        for e in range(chips):
+            gather_core[t, d, e].wait_recv()
+        if t == 0 and d > 0:
+            left_in[d].wait_recv()
+        left = left_ops if d == 0 else left_recv[d - 1]
+
+        def one(k, carry):
+            block = recv_block[d * slots + k]
+            right_matrix = right_ops[block_right[block]]
+            left_matrix = left[block_left[block]]
+            middle = lax.dot_general(
+                values[t, d, k],
+                right_matrix,
+                (((1,), (1,)), ((), ())),
+                preferred_element_type=jnp.float32,
+            ).astype(jnp.bfloat16)
+            partial[t, d, k] = jnp.dot(
+                left_matrix, middle, preferred_element_type=jnp.float32
+            ).astype(jnp.bfloat16)
+            return carry
+
+        lax.fori_loop(0, slots, one, 0, unroll=True)
+        for e in range(chips):
+            reduce_core[t, d, e] = remote(
+                partial.at[t, d, :, share_rows(chip_at[e], 1 - core), :],
+                from_core.at[t, d, e],
+                rsc_send.at[t, d, e],
+                rsc_recv.at[t, d, e],
+                partner,
+            )
+
+    def chip_sum(t, d, e, k):
+        mine = partial[t, d, k, share_rows(chip_at[e], core), :].astype(jnp.float32)
+        return mine + from_core[t, d, e, k].astype(jnp.float32)
+
+    def reduce_pass(t, d):
+        for e in range(chips):
+            reduce_core[t, d, e].wait_recv()
+        for e in range(1, chips):
+
+            def one(k, carry):
+                to_chip[t, d, e, k] = chip_sum(t, d, e, k).astype(jnp.bfloat16)
+                return carry
+
+            lax.fori_loop(0, slots, one, 0, unroll=True)
+            reduce_chip[t, d, e] = remote(
+                to_chip.at[t, d, e],
+                from_chip.at[t, d, e],
+                rsx_send.at[t, d, e],
+                rsx_recv.at[t, d, e],
+                chip_peer[e],
+            )
+
+    def finish(t, d):
+        for e in range(1, chips):
+            reduce_chip[t, d, e].wait_recv()
+
+        def one(k, carry):
+            total = chip_sum(t, d, 0, k)
+            for e in range(1, chips):
+                total = total + from_chip[t, d, e, k].astype(jnp.float32)
+            block = recv_block[d * slots + k]
+            row_limit = left_dims[sec_after[d] * left_per + block_left[block]]
+            col_limit = right_dims[me * right_per + block_right[block]]
+            live = (row_ids < row_limit) & (col_ids < col_limit)
+            total = jnp.where(live, total, 0.0).astype(jnp.bfloat16)
+            if t == 0:
+                values[1, d, k, own_rows, :] = total
+            if d == 0:
+                returned[t][0, k] = total
+            elif t == 1:
+                final[d, k] = total
+            return carry
+
+        lax.fori_loop(0, slots, one, 0, unroll=True)
+        if t == 0:
+            gather_start(1, d)
+        if d > 0:
+            place = senders - d
+            back[t, d] = remote(
+                values.at[1, d, :, own_rows, :] if t == 0 else final.at[d],
+                returned[t].at[place],
+                z_send.at[2 + t, d],
+                z_recv.at[2 + t, place],
+                {"sec": sec_after[d]},
+            )
+
+    def give(t, d):
+        for e in range(1, senders):
+            back[t, e].wait_recv()
+        out = (out_first, out_second)[t]
+
+        def one(b, carry):
+            place = send_place[b]
+            out[b] = returned[t][place // slots, place % slots]
+            return carry
+
+        lax.fori_loop(0, blocks, one, 0)
+
+    steps = []
+    for d in range(senders):
+        chain = [(gather_start, 0)]
+        for t in (0, 1):
+            chain += [(gather_pass, t), (apply, t), (reduce_pass, t), (finish, t)]
+        steps += [(SKEW * d + i, d, f, t) for i, (f, t) in enumerate(chain)]
+    for _, d, f, t in sorted(steps, key=lambda s: (s[0], s[1])):
+        f(t, d)
+    give(0, 0)
+    give(1, 0)
+    for copy in sent:
+        copy.wait_send()
+
+
+def fused_body(
+    psi, left_ops, right_ops, left_dims, right_dims, block_left, block_right, right_owner
+):
+    senders = lax.axis_size("sec")
+    holders = lax.axis_size("op")
+    me = lax.axis_index("sec")
+    blocks, rows, cols = psi.shape
+    slots = -(-blocks // senders)
+    share = rows // holders
+    chips = holders // CORES
+    left_per = left_ops.shape[1]
+
+    owner = right_owner.reshape(senders, blocks)
+    ids = jnp.arange(blocks, dtype=jnp.int32)
+    same = (owner[:, :, None] == owner[:, None, :]) & (ids[None, None, :] < ids[None, :, None])
+    rank = jnp.sum(same.astype(jnp.int32), axis=2)
+    offsets = jnp.arange(senders, dtype=jnp.int32)
+    slot_ids = jnp.arange(slots, dtype=jnp.int32)
+    mine_owner = lax.dynamic_index_in_dim(owner, me, 0, keepdims=False)
+    mine_rank = lax.dynamic_index_in_dim(rank, me, 0, keepdims=False)
+    send_to = (me - offsets + senders) % senders
+    send_pick = (mine_owner[None, None, :] == send_to[:, None, None]) & (
+        mine_rank[None, None, :] == slot_ids[None, :, None]
+    )
+    send_block = jnp.sum(jnp.where(send_pick, ids[None, None, :], 0), axis=2).reshape(-1)
+    sender_ids = offsets[:, None]
+    global_ids = sender_ids * blocks + ids[None, :]
+    from_sec = (me + offsets) % senders
+    recv_pick = (
+        (owner == me)[None, None]
+        & (rank[None, None] == slot_ids[None, :, None, None])
+        & (sender_ids[None, None] == from_sec[:, None, None, None])
+    )
+    recv_block = jnp.sum(jnp.where(recv_pick, global_ids[None, None], 0), axis=(2, 3)).reshape(-1)
+    send_place = ((mine_owner - me + senders) % senders) * slots + mine_rank
+
+    smem = pl.BlockSpec(memory_space=pltpu.SMEM)
+    vmem = pl.BlockSpec(memory_space=pltpu.VMEM)
+    dma = pltpu.SemaphoreType.DMA
+    bf = jnp.bfloat16
+    result = jax.ShapeDtypeStruct((blocks, share, cols), bf)
+    parts = (2, senders, chips, slots, share, cols)
+    grid = (2, senders, chips)
+    return pl.pallas_call(
+        functools.partial(kernel, senders, holders),
+        out_shape=(result, result),
+        in_specs=[smem] * 7 + [vmem] * 3,
+        out_specs=(vmem, vmem),
+        scratch_shapes=[
+            pltpu.VMEM((senders, slots, share, cols), bf),
+            pltpu.VMEM((2, senders, slots, rows, cols), bf),
+            pltpu.VMEM((2, senders, slots, rows, cols), bf),
+            pltpu.VMEM(parts, bf),
+            pltpu.VMEM(parts, bf),
+            pltpu.VMEM(parts, bf),
+            pltpu.VMEM((senders, slots, share, cols), bf),
+            pltpu.VMEM((senders, slots, share, cols), bf),
+            pltpu.VMEM((senders, slots, share, cols), bf),
+            dma((4, senders)),
+            dma((4, senders)),
+        ]
+        + [dma(grid)] * 8
+        + [pltpu.VMEM(left_ops.shape[1:], bf)] * (senders - 1),
+        compiler_params=pltpu.CompilerParams(
+            collective_id=0, has_side_effects=True, vmem_limit_bytes=VMEM_BUDGET
+        ),
+        cost_estimate=pl.CostEstimate(
+            flops=4 * blocks * rows * cols * (rows + cols),
+            bytes_accessed=8 * blocks * rows * cols,
+            transcendentals=0,
+        ),
+    )(
+        send_block,
+        recv_block,
+        send_place,
+        left_dims,
+        right_dims,
+        block_left,
+        block_right,
+        psi,
+        left_ops[0],
+        right_ops[0],
+    )
+
+
+def any_body(psi, left_ops, right_ops, *tables):
+    senders = lax.axis_size("sec")
+    whole = 2 * (6 * psi.size + senders * left_ops.size + right_ops.size)
+    if whole * 5 // 4 < VMEM_BUDGET and lax.axis_size("op") % CORES == 0:
+        return fused_body(psi, left_ops, right_ops, *tables)
+    return body(psi, left_ops, right_ops, *tables)
+
+
 def solution(mesh):
     return jax.shard_map(
-        body,
+        any_body,
         mesh=mesh,
         in_specs=(
             P(("groups", "sec"), None, None),

time: 209 us -> 90.1 us (0.43)
  waiting for transfers between devices: 159 us -> 0 us
  Pallas kernels: 0 us -> 78.2 us
  between operations: 13.9 us -> 0.69 us
  matrix products: 11.5 us -> 0 us
  starting transfers between devices: 6.55 us -> 0 us
  other arithmetic: 7.23 us -> 1.78 us
    all_to_all x1 -> x0, waiting for transfers between devices: 79.4 us -> none  [body(): lax.all_to_all(right_matrices, 'sec', split_axis=0, concat_axis=0, tiled=...]
    pallas_call x0 -> x1, Pallas kernels: none -> 78.2 us  [fused_body(): pl.pallas_call(functools.partial(kernel, senders, holders), out_shape=(re...]
    reduce_scatter x2 -> x0, waiting for transfers between devices: 58.2 us -> none  [the longest x1 30 us: body(): lax.psum_scatter(second_terms.astype(jnp.float32).astype(jnp.bfloat16), '...]
    all_gather x1 -> x0, waiting for transfers between devices: 21.4 us -> none  [op_combine(): full_sigma = lax.all_gather(own_rows, 'op', axis=1, tiled=True)]
    dot_general x2 -> x0, matrix products: 11.5 us -> none  [the longest x1 5.78 us: right_apply(): jnp.einsum('prc,pdc->prd', values, matrices, preferred_element_type=jnp.f...]
    gather x5 -> x0, local copies, waits for them, and re-layouts: 9.42 us -> none  [the longest x1 4.67 us: body(): mine_matrices = jnp.take(operators_back, send_pos, axis=0)]
    unnamed x12 -> x16, local copies, waits for them, and re-layouts: 0.04 us -> 7.78 us
    all_to_all x1 -> x0, starting transfers between devices: 6.46 us -> none  [body(): lax.all_to_all(right_matrices, 'sec', split_axis=0, concat_axis=0, tiled=...]
  transfers between devices with their start and end apart: 4 -> 0, of which waited for: 4 -> 0; matrix products, arithmetic and copies ran while one was open for 2% -> 0% of each run, Pallas kernels for 0% -> 0%
where the time goes in v1:
time: 90.1 us; the launch traced here: 89.8 us
  Pallas kernels  78.2 us (87%)
  local copies, waits for them, and re-layouts  9.15 us (10%)
  other arithmetic  1.78 us (2%)
    pallas_call x1, Pallas kernels, fused_body(): pl.pallas_call(functools.partial(kernel, senders, holders), out_shape=(re...  78.2 us
    unnamed x16, local copies, waits for them, and re-layouts  7.78 us

profile of v1, /device:TPU:0, one launch (start us, length us, event | category | flops | bytes accessed | tf_op | source)
XLA Modules:
  0.0 89.8 jit_solution(622794305803651521)
XLA Ops:
  0.7 0.1 iota_compare_fusion.3
  0.7 0.1 iota_add_fusion
  0.8 0.7 reshape.187
  1.6 0.1 copy.13
  1.7 0.6 convert_reduce_fusion
  2.3 0.2 dynamic-slice_reduce_fusion
  2.5 0.1 copy.15
  2.6 0.1 broadcast_compare_fusion.1
  2.7 0.7 select_reduce_fusion
  3.3 0.1 reshape.189.recv_block
  3.4 0.2 select_reduce_fusion.1
  3.6 0.1 copy.14
  3.7 0.1 reshape.188.send_block
  3.8 0.0 copy-start
  3.8 1.5 %copy-done = bf16[28,128,256]{2,1,0:T(8,128)(2,1)S(1)} copy-done((bf16[28,128,256]{2,1,0:T(8,128)(2,1)S(1)}, bf16[28,128,256]{2,1,0:T(8,128)(2,1)}, u32[]{:S(2)}) %copy-start) | copy-done | bytes 1835032
  5.3 0.0 copy-start.1
  5.3 1.2 %copy-done.1 = bf16[1,7,256,256]{3,2,1,0:T(8,128)(2,1)S(1)} copy-done((bf16[1,7,256,256]{3,2,1,0:T(8,128)(2,1)S(1)}, bf16[1,7,256,256]{3,2,1,0:T(8,128)(2,1)}, u32[]{:S(2)}) %copy-start.1) | copy-done | bytes 917528
  6.5 0.0 copy-start.2
  6.5 0.9 %copy-done.2 = bf16[1,7,128,128]{3,2,1,0:T(8,128)(2,1)S(1)} copy-done((bf16[1,7,128,128]{3,2,1,0:T(8,128)(2,1)S(1)}, bf16[1,7,128,128]{3,2,1,0:T(8,128)(2,1)}, u32[]{:S(2)}) %copy-start.2) | copy-done | bytes 229400
  7.4 0.0 copy-start.3
  7.4 0.7 copy-done.3
  8.1 0.0 copy-start.4
  8.1 0.7 copy-done.4
  8.8 0.0 copy-start.5
  8.8 0.7 copy-done.5
  9.4 0.0 copy-start.6
  9.4 0.7 copy-done.6
  10.1 78.2 %shard_map.95 = (bf16[28,32,256]{2,1,0:T(8,128)(2,1)S(1)}, bf16[28,32,256]{2,1,0:T(8,128)(2,1)S(1)}) custom-call(s32[28]{0:T(128)S(1)} %reshape.188.send_block, s32[28]{0:T(128)S(1)} %reshape.189.recv_block, s32[28]{0:T(128)S(1)} %get-tuple-element.2.send_place, s32[28]{0:T(128)S(1)} %copy-done.3, s32[28]{0:T(128)S(1)} %copy-done.4, s32[112]{0:T(128)S(1)} %copy-done.5, ...), custom_call_target="tpu_custom_call" | custom-call | flops 1409286144 | bytes 7340032 | tf_op jit(solution)/shard_map/pallas_call | solution.py:394
  88.3 0.8 copy.18
  89.1 0.8 copy.19
  (7 shorter events, 0.1 us)
Async XLA Ops:
  3.8 1.5 %copy-start = (bf16[28,128,256]{2,1,0:T(8,128)(2,1)S(1)}, bf16[28,128,256]{2,1,0:T(8,128)(2,1)}, u32[]{:S(2)}) copy-start(bf16[28,128,256]{2,1,0:T(8,128)(2,1)} %psi.1) | copy-start | bytes 5505028
  5.3 1.2 %copy-start.1 = (bf16[1,7,256,256]{3,2,1,0:T(8,128)(2,1)S(1)}, bf16[1,7,256,256]{3,2,1,0:T(8,128)(2,1)}, u32[]{:S(2)}) copy-start(bf16[1,7,256,256]{3,2,1,0:T(8,128)(2,1)} %param.10) | copy-start | bytes 2752516
  6.5 0.9 %copy-start.2 = (bf16[1,7,128,128]{3,2,1,0:T(8,128)(2,1)S(1)}, bf16[1,7,128,128]{3,2,1,0:T(8,128)(2,1)}, u32[]{:S(2)}) copy-start(bf16[1,7,128,128]{3,2,1,0:T(8,128)(2,1)} %param.9) | copy-start | bytes 688132
  7.4 0.7 copy-start.3
  8.1 0.7 copy-start.4
  8.8 0.7 copy-start.5
  9.4 0.7 copy-start.6

commit v2 on v1

--- a/solution.py
+++ b/solution.py
@@ -90,8 +90,15 @@
 
 MESH = pl.DeviceIdType.MESH
 CORES = 2
-SKEW = 2
 VMEM_BUDGET = 40 * 2**20
+
+
+def pair(a, b, count):
+    out, bit = 0, 1
+    while bit < count:
+        out = out + (a // bit + b // bit) % 2 * bit
+        bit *= 2
+    return out
 
 
 def kernel(
@@ -100,6 +107,15 @@
     send_block,
     recv_block,
     send_place,
+    left_dims_hbm,
+    right_dims_hbm,
+    block_left_hbm,
+    block_right_hbm,
+    psi_hbm,
+    left_hbm,
+    right_hbm,
+    out_first,
+    out_second,
     left_dims,
     right_dims,
     block_left,
@@ -107,8 +123,7 @@
     psi,
     left_ops,
     right_ops,
-    out_first,
-    out_second,
+    fetch_sem,
     packed,
     values,
     partial,
@@ -134,7 +149,7 @@
     op = lax.axis_index("op")
     chips = holders // CORES
     chip, core = op // CORES, op % CORES
-    blocks, rows, cols = psi.shape
+    blocks, rows, cols = psi_hbm.shape
     left_per, right_per = left_ops.shape[0], right_ops.shape[0]
     slots = values.shape[2]
     share = rows // holders
@@ -148,11 +163,27 @@
     partner = {"op": chip * CORES + (1 - core)}
     chip_at = [lax.rem(chip + e, chips) for e in range(chips)]
     chip_peer = [{"op": c * CORES + core} for c in chip_at]
-    sec_before = [lax.rem(me - d + senders, senders) for d in range(senders)]
-    sec_after = [lax.rem(me + d, senders) for d in range(senders)]
+    sec_at = [pair(me, d, senders) for d in range(senders)]
+
+    fetches = [
+        pltpu.make_async_copy(src, dst, fetch_sem.at[i])
+        for i, (src, dst) in enumerate(
+            (
+                (psi_hbm.at[:, own_rows, :], psi),
+                (left_dims_hbm, left_dims),
+                (right_dims_hbm, right_dims),
+                (block_left_hbm, block_left),
+                (block_right_hbm, block_right),
+                (left_hbm, left_ops),
+                (right_hbm, right_ops),
+            )
+        )
+    ]
+    for fetch in fetches:
+        fetch.start()
 
     barrier = pltpu.get_barrier_semaphore()
-    peers = [{"sec": sec_before[d]} for d in range(1, senders)] + [partner] + chip_peer[1:]
+    peers = [{"sec": sec_at[d]} for d in range(1, senders)] + [partner] + chip_peer[1:]
     for peer in peers:
         pl.semaphore_signal(barrier, inc=1, device_id=peer, device_id_type=MESH)
 
@@ -162,10 +193,10 @@
     def pack(d):
         def one(k, carry):
             block = send_block[d * slots + k]
-            value = psi[block, own_rows, :].astype(jnp.float32)
+            value = psi[block].astype(jnp.float32)
             gb = me * blocks + block
             row_limit = left_dims[me * left_per + block_left[gb]]
-            col_limit = right_dims[sec_before[d] * right_per + block_right[gb]]
+            col_limit = right_dims[sec_at[d] * right_per + block_right[gb]]
             live = (row_ids < row_limit) & (col_ids < col_limit)
             value = jnp.where(live, value, 0.0).astype(jnp.bfloat16)
             if d == 0:
@@ -200,23 +231,38 @@
         {},
     )
 
-    for d in range(senders):
+    def send_left(d):
+        if 0 < d < senders:
+            left_in[d] = remote(
+                left_hbm,
+                left_recv[d - 1],
+                z_send.at[1, d],
+                z_recv.at[1, d],
+                {"sec": sec_at[d]},
+            )
+
+    for fetch in fetches[:5]:
+        fetch.wait()
+    for d in range(1, senders):
         pack(d)
     pl.semaphore_wait(barrier, len(peers))
     for d in range(1, senders):
-        to = {"sec": sec_before[d]}
         inbound[d] = remote(
             packed.at[d],
             values.at[0, d, :, own_rows, :],
             z_send.at[0, d],
             z_recv.at[0, d],
-            to,
+            {"sec": sec_at[d]},
         )
-        left_in[d] = remote(left_ops, left_recv[d - 1], z_send.at[1, d], z_recv.at[1, d], to)
+        if d == 1:
+            send_left(1)
+    pack(0)
 
     def gather_start(t, d):
         if t == 0 and d > 0:
             inbound[d].wait_recv()
+        if t == 0 and d == 2:
+            send_left(2)
         part = values.at[t, d, :, own_rows, :]
         for e in range(1, chips):
             gather_chip[t, d, e] = remote(
@@ -237,8 +283,13 @@
     def apply(t, d):
         for e in range(chips):
             gather_core[t, d, e].wait_recv()
+        if t == 0 and d == 0:
+            fetches[5].wait()
+            fetches[6].wait()
         if t == 0 and d > 0:
             left_in[d].wait_recv()
+            if d + 2 > 2:
+                send_left(d + 2)
         left = left_ops if d == 0 else left_recv[d - 1]
 
         def one(k, carry):
@@ -297,7 +348,7 @@
             for e in range(1, chips):
                 total = total + from_chip[t, d, e, k].astype(jnp.float32)
             block = recv_block[d * slots + k]
-            row_limit = left_dims[sec_after[d] * left_per + block_left[block]]
+            row_limit = left_dims[sec_at[d] * left_per + block_left[block]]
             col_limit = right_dims[me * right_per + block_right[block]]
             live = (row_ids < row_limit) & (col_ids < col_limit)
             total = jnp.where(live, total, 0.0).astype(jnp.bfloat16)
@@ -313,13 +364,13 @@
         if t == 0:
             gather_start(1, d)
         if d > 0:
-            place = senders - d
+            place = d
             back[t, d] = remote(
                 values.at[1, d, :, own_rows, :] if t == 0 else final.at[d],
                 returned[t].at[place],
                 z_send.at[2 + t, d],
                 z_recv.at[2 + t, place],
-                {"sec": sec_after[d]},
+                {"sec": sec_at[d]},
             )
 
     def give(t, d):
@@ -336,10 +387,13 @@
 
     steps = []
     for d in range(senders):
-        chain = [(gather_start, 0)]
+        steps += [(d, d, gather_start, 0), (d + 1.5, d, gather_pass, 0)]
+        at = 2 + 3 * d
         for t in (0, 1):
-            chain += [(gather_pass, t), (apply, t), (reduce_pass, t), (finish, t)]
-        steps += [(SKEW * d + i, d, f, t) for i, (f, t) in enumerate(chain)]
+            if t == 1:
+                steps.append((at + 6, d, gather_pass, 1))
+            start = at + 8 * t
+            steps += [(start + 2 * i, d, f, t) for i, f in enumerate((apply, reduce_pass, finish))]
     for _, d, f, t in sorted(steps, key=lambda s: (s[0], s[1])):
         f(t, d)
     give(0, 0)
@@ -368,24 +422,25 @@
     slot_ids = jnp.arange(slots, dtype=jnp.int32)
     mine_owner = lax.dynamic_index_in_dim(owner, me, 0, keepdims=False)
     mine_rank = lax.dynamic_index_in_dim(rank, me, 0, keepdims=False)
-    send_to = (me - offsets + senders) % senders
+    send_to = pair(me, offsets, senders)
     send_pick = (mine_owner[None, None, :] == send_to[:, None, None]) & (
         mine_rank[None, None, :] == slot_ids[None, :, None]
     )
     send_block = jnp.sum(jnp.where(send_pick, ids[None, None, :], 0), axis=2).reshape(-1)
     sender_ids = offsets[:, None]
     global_ids = sender_ids * blocks + ids[None, :]
-    from_sec = (me + offsets) % senders
+    from_sec = send_to
     recv_pick = (
         (owner == me)[None, None]
         & (rank[None, None] == slot_ids[None, :, None, None])
         & (sender_ids[None, None] == from_sec[:, None, None, None])
     )
     recv_block = jnp.sum(jnp.where(recv_pick, global_ids[None, None], 0), axis=(2, 3)).reshape(-1)
-    send_place = ((mine_owner - me + senders) % senders) * slots + mine_rank
+    send_place = pair(me, mine_owner, senders) * slots + mine_rank
 
     smem = pl.BlockSpec(memory_space=pltpu.SMEM)
     vmem = pl.BlockSpec(memory_space=pltpu.VMEM)
+    hbm = pl.BlockSpec(memory_space=pl.ANY)
     dma = pltpu.SemaphoreType.DMA
     bf = jnp.bfloat16
     result = jax.ShapeDtypeStruct((blocks, share, cols), bf)
@@ -394,9 +449,17 @@
     return pl.pallas_call(
         functools.partial(kernel, senders, holders),
         out_shape=(result, result),
-        in_specs=[smem] * 7 + [vmem] * 3,
+        in_specs=[smem] * 3 + [hbm] * 7,
         out_specs=(vmem, vmem),
         scratch_shapes=[
+            pltpu.SMEM(left_dims.shape, jnp.int32),
+            pltpu.SMEM(right_dims.shape, jnp.int32),
+            pltpu.SMEM(block_left.shape, jnp.int32),
+            pltpu.SMEM(block_right.shape, jnp.int32),
+            pltpu.VMEM((blocks, share, cols), bf),
+            pltpu.VMEM(left_ops.shape[1:], bf),
+            pltpu.VMEM(right_ops.shape[1:], bf),
+            dma((7,)),
             pltpu.VMEM((senders, slots, share, cols), bf),
             pltpu.VMEM((2, senders, slots, rows, cols), bf),
             pltpu.VMEM((2, senders, slots, rows, cols), bf),
@@ -436,7 +499,7 @@
 def any_body(psi, left_ops, right_ops, *tables):
     senders = lax.axis_size("sec")
     whole = 2 * (6 * psi.size + senders * left_ops.size + right_ops.size)
-    if whole * 5 // 4 < VMEM_BUDGET and lax.axis_size("op") % CORES == 0:
+    if whole * 5 // 4 < VMEM_BUDGET and lax.axis_size("op") % CORES == 0 and senders & (senders - 1) == 0:
         return fused_body(psi, left_ops, right_ops, *tables)
     return body(psi, left_ops, right_ops, *tables)
 

time: 90.1 us -> 84.9 us (0.942)
  Pallas kernels: 78.2 us -> 73 us
    pallas_call x1, Pallas kernels: 78.2 us -> 73 us  [fused_body(): pl.pallas_call(functools.partial(kernel, senders, holders), out_shape=(re...]
where the time goes in v2:
time: 84.9 us; the launch traced here: 84.6 us
  Pallas kernels  73 us (86%)
  local copies, waits for them, and re-layouts  9.15 us (11%)
  other arithmetic  1.79 us (2%)
    pallas_call x1, Pallas kernels, fused_body(): pl.pallas_call(functools.partial(kernel, senders, holders), out_shape=(re...  73 us
    unnamed x16, local copies, waits for them, and re-layouts  7.78 us

profile of v2, /device:TPU:0, one launch (start us, length us, event | category | flops | bytes accessed | tf_op | source)
XLA Modules:
  0.0 84.6 jit_solution(5611602263386032915)
XLA Ops:
  0.7 0.1 iota_compare_fusion.3
  0.7 0.1 iota_add_fusion
  0.8 0.7 reshape.236
  1.6 0.1 copy.13
  1.7 0.6 convert_reduce_fusion
  2.3 0.2 dynamic-slice_reduce_fusion
  2.5 0.1 copy.15
  2.6 0.1 broadcast_compare_fusion.1
  2.7 0.7 select_reduce_fusion
  3.3 0.1 reshape.238.recv_block
  3.4 0.2 select_reduce_fusion.1
  3.7 0.1 copy.14
  3.7 0.1 reshape.237.send_block
  3.8 0.0 copy-start
  3.8 1.5 %copy-done = bf16[28,128,256]{2,1,0:T(8,128)(2,1)S(1)} copy-done((bf16[28,128,256]{2,1,0:T(8,128)(2,1)S(1)}, bf16[28,128,256]{2,1,0:T(8,128)(2,1)}, u32[]{:S(2)}) %copy-start) | copy-done | bytes 1835032
  5.3 0.0 copy-start.1
  5.3 1.2 %copy-done.1 = bf16[1,7,256,256]{3,2,1,0:T(8,128)(2,1)S(1)} copy-done((bf16[1,7,256,256]{3,2,1,0:T(8,128)(2,1)S(1)}, bf16[1,7,256,256]{3,2,1,0:T(8,128)(2,1)}, u32[]{:S(2)}) %copy-start.1) | copy-done | bytes 917528
  6.5 0.0 copy-start.2
  6.5 0.9 %copy-done.2 = bf16[1,7,128,128]{3,2,1,0:T(8,128)(2,1)S(1)} copy-done((bf16[1,7,128,128]{3,2,1,0:T(8,128)(2,1)S(1)}, bf16[1,7,128,128]{3,2,1,0:T(8,128)(2,1)}, u32[]{:S(2)}) %copy-start.2) | copy-done | bytes 229400
  7.5 0.0 copy-start.3
  7.5 0.7 copy-done.3
  8.1 0.0 copy-start.4
  8.1 0.7 copy-done.4
  8.8 0.0 copy-start.5
  8.8 0.7 copy-done.5
  9.4 0.0 copy-start.6
  9.4 0.7 copy-done.6
  10.1 73.0 %shard_map.95 = (bf16[28,32,256]{2,1,0:T(8,128)(2,1)S(1)}, bf16[28,32,256]{2,1,0:T(8,128)(2,1)S(1)}) custom-call(s32[28]{0:T(128)S(1)} %reshape.237.send_block, s32[28]{0:T(128)S(1)} %reshape.238.recv_block, s32[28]{0:T(128)S(1)} %get-tuple-element.2.send_place, s32[28]{0:T(128)S(1)} %copy-done.3, s32[28]{0:T(128)S(1)} %copy-done.4, s32[112]{0:T(128)S(1)} %copy-done.5, ...), custom_call_target="tpu_custom_call" | custom-call | flops 1409286144 | bytes 7340032 | tf_op jit(solution)/shard_map/pallas_call | solution.py:449
  83.1 0.8 copy.18
  83.8 0.8 copy.19
  (7 shorter events, 0.1 us)
Async XLA Ops:
  3.8 1.5 %copy-start = (bf16[28,128,256]{2,1,0:T(8,128)(2,1)S(1)}, bf16[28,128,256]{2,1,0:T(8,128)(2,1)}, u32[]{:S(2)}) copy-start(bf16[28,128,256]{2,1,0:T(8,128)(2,1)} %psi_hbm.1) | copy-start | bytes 5505028
  5.3 1.2 %copy-start.1 = (bf16[1,7,256,256]{3,2,1,0:T(8,128)(2,1)S(1)}, bf16[1,7,256,256]{3,2,1,0:T(8,128)(2,1)}, u32[]{:S(2)}) copy-start(bf16[1,7,256,256]{3,2,1,0:T(8,128)(2,1)} %param.10) | copy-start | bytes 2752516
  6.5 0.9 %copy-start.2 = (bf16[1,7,128,128]{3,2,1,0:T(8,128)(2,1)S(1)}, bf16[1,7,128,128]{3,2,1,0:T(8,128)(2,1)}, u32[]{:S(2)}) copy-start(bf16[1,7,128,128]{3,2,1,0:T(8,128)(2,1)} %param.9) | copy-start | bytes 688132
  7.5 0.7 copy-start.3
  8.1 0.7 copy-start.4
  8.8 0.7 copy-start.5
  9.4 0.7 copy-start.6

commit v3 on v2

--- a/solution.py
+++ b/solution.py
@@ -91,6 +91,7 @@
 MESH = pl.DeviceIdType.MESH
 CORES = 2
 VMEM_BUDGET = 40 * 2**20
+VMEM_LIMIT = 62 * 2**20
 
 
 def pair(a, b, count):
@@ -475,7 +476,7 @@
         + [dma(grid)] * 8
         + [pltpu.VMEM(left_ops.shape[1:], bf)] * (senders - 1),
         compiler_params=pltpu.CompilerParams(
-            collective_id=0, has_side_effects=True, vmem_limit_bytes=VMEM_BUDGET
+            collective_id=0, has_side_effects=True, vmem_limit_bytes=VMEM_LIMIT
         ),
         cost_estimate=pl.CostEstimate(
             flops=4 * blocks * rows * cols * (rows + cols),

time: 84.9 us -> 82.8 us (0.975)
  local copies, waits for them, and re-layouts: 9.15 us -> 6.06 us
    unnamed x16 -> x2, local copies, waits for them, and re-layouts: 7.78 us -> 3.63 us
where the time goes in v3:
time: 82.8 us; the launch traced here: 82.5 us
  Pallas kernels  73.5 us (89%)
  local copies, waits for them, and re-layouts  6.06 us (7%)
  other arithmetic  2.3 us (3%)
    pallas_call x1, Pallas kernels, fused_body(): pl.pallas_call(functools.partial(kernel, senders, holders), out_shape=(re...  73.5 us
    unnamed x2, local copies, waits for them, and re-layouts  3.63 us

profile of v3, /device:TPU:0, one launch (start us, length us, event | category | flops | bytes accessed | tf_op | source)
XLA Modules:
  0.0 82.5 jit_solution(17881032913677729828)
XLA Ops:
  0.7 0.1 iota_compare_fusion.3
  0.7 0.1 iota_add_fusion
  0.8 0.7 reshape.236
  1.6 0.1 copy.13
  1.7 0.6 convert_reduce_fusion
  2.3 0.2 dynamic-slice_reduce_fusion
  2.5 0.1 copy.15
  2.6 0.5 multiply_add_fusion
  3.1 0.1 broadcast_compare_fusion.1
  3.2 0.7 select_reduce_fusion
  3.9 0.6 reshape.238.recv_block
  4.5 0.2 select_reduce_fusion.1
  4.7 0.1 copy.14
  4.8 0.6 reshape.237.send_block
  5.4 73.5 %shard_map.95 = (bf16[28,32,256]{2,1,0:T(8,128)(2,1)}, bf16[28,32,256]{2,1,0:T(8,128)(2,1)}) custom-call(s32[28]{0:T(128)} %reshape.237.send_block, s32[28]{0:T(128)} %reshape.238.recv_block, s32[28]{0:T(128)} %get-tuple-element.2.send_place, s32[28]{0:T(128)} %left_dims_hbm.1, s32[28]{0:T(128)} %right_dims_hbm.1, s32[112]{0:T(128)} %block_left_hbm.1, ...), custom_call_target="tpu_custom_call" | custom-call | flops 1409286144 | bytes 7340032 | tf_op jit(solution)/shard_map/pallas_call | solution.py:450
  78.9 1.8 %copy.18 = bf16[28,32,256]{2,1,0:T(8,128)(2,1)} copy(bf16[28,32,256]{2,1,0:T(8,128)(2,1)} %get-tuple-element.6) | data formatting | bytes 917504
  80.7 1.8 %copy.19 = bf16[28,32,256]{2,1,0:T(8,128)(2,1)} copy(bf16[28,32,256]{2,1,0:T(8,128)(2,1)} %get-tuple-element.7) | data formatting | bytes 917504
  (6 shorter events, 0.0 us)
